TPU v7x, 256 devices: a whole 4x4x8 slice. The times are simulated.
256 devices in a mesh: ctx: 32 (over z, x), dp: 8 (over y, core).
Axes of the slice: x: 4, y: 4, z: 8, core: 2. Of those that a mesh axis runs over, the one named last changes fastest.
Arguments:
- mel_frames: bfloat16 [8, 4096, 128], P('dp', 'ctx'), may hold values from -6 to 6
- conv_weight: bfloat16 [384, 1280], replicated, may hold values from -0.3125 to 0.3125
- conv_bias: float32 [1280], replicated, may hold values from -3 to 3
- video_hidden: bfloat16 [8, 4096, 5120], P('dp', 'ctx'), may hold values from -6 to 6
- video_count: int32 [8, 32], P('dp', 'ctx'), may hold values from 0 to 128, as said below
- video_places: int32 [8, 4096], P('dp', 'ctx'), may hold values from 0 to 6143, as said below
- audio_places: int32 [8, 4096], P('dp', 'ctx'), may hold values from 0 to 6143, as said below
- cotangent: bfloat16 [8, 6144, 3584], P('dp', 'ctx'), may hold values from -0.049804688 to 0.049804688
Outputs:
- grad_merger: float32 [32, 640, 896], P('ctx', 'dp')
- grad_audio: float32 [32, 160, 896], P('ctx', 'dp')
Inputs may be any that keep to these rules, and one draw needn't show every extreme that they name: `video_count`: in every sequence, shards 2i and 2i + 1 of encoder time hold 128 live video rows together, and some shard holds 128. `video_places`: in each sequence the live video slots (slot index within its shard below the shard's count) and the audio rows name every position exactly once; slots at or past the count hold arbitrary positions. `audio_places`: see video_places.
All inputs are finite; a program needn't handle non-finite values.
Results may differ from a plain program's by a relative error of at most 0.0029.
Values may be sent and summed in bfloat16 or wider, within the bound.
A program may use at most 128 MiB of HBM per device.

v0:
```python
import jax
import jax.numpy as jnp
from jax import lax
from jax.sharding import Mesh, PartitionSpec as P

GRID_ROWS = 8
GRID_COLS = 4


def local(
    mel, conv_weight, conv_bias, video_hidden, video_count, video_places, audio_places, cotangent
):
    z = lax.axis_index("z")
    hidden = video_hidden[0]
    places = video_places[0]
    upstream = cotangent[0]
    block_cols = upstream.shape[1] // GRID_COLS
    enc = conv_weight.shape[1] // GRID_ROWS
    cols = lax.all_to_all(
        jnp.transpose(upstream.reshape(-1, GRID_COLS, block_cols), (1, 0, 2)), "x", 0, 0, tiled=True
    )
    up = lax.all_gather(cols, "z", tiled=True).reshape(-1, block_cols)
    live_count = video_count[0, 0]
    middle = hidden.shape[0] // 2
    pairs = [(i, i ^ 1) for i in range(lax.axis_size("x"))]
    got_rows, got_places = lax.ppermute((hidden[middle:], places[middle:]), "x", pairs)
    joined = jnp.concatenate([hidden[:middle], got_rows], axis=0)
    joined_places = jnp.concatenate([places[:middle], got_places], axis=0)
    ids = jnp.arange(middle, dtype=jnp.int32)
    source = jnp.where((ids < live_count) | (live_count >= middle), ids, middle + ids - live_count)
    rows = jnp.take(joined, source, axis=0)
    spots = jnp.take(joined_places, source, axis=0)
    rows = lax.all_to_all(
        jnp.transpose(rows.reshape(middle, GRID_ROWS, -1), (1, 0, 2)), "z", 0, 0, tiled=True
    )
    rows = lax.all_gather(rows, "x", axis=1, tiled=False)
    rows = rows.reshape(-1, rows.shape[-1])
    spots = lax.all_gather(lax.all_gather(spots, "x"), "z").reshape(-1)
    frames = lax.all_gather(lax.all_gather(mel[0], "x"), "z").reshape(-1, mel.shape[-1])
    audio_spots = lax.all_gather(lax.all_gather(audio_places[0], "x"), "z").reshape(-1)
    pad = jnp.zeros((1, frames.shape[1]), frames.dtype)
    padded = jnp.concatenate([pad, frames, pad], axis=0)
    windows = jnp.concatenate([padded[:-2], padded[1:-1], padded[2:]], axis=1)
    weight = lax.dynamic_slice_in_dim(conv_weight, z * enc, enc, axis=1)
    bias = lax.dynamic_slice_in_dim(conv_bias, z * enc, enc, axis=0)
    conv = jnp.dot(windows, weight, preferred_element_type=jnp.float32) + bias
    audio = jax.nn.gelu(conv, approximate=False).astype(jnp.bfloat16)
    contract = (((0,), (0,)), ((), ()))
    merger = lax.dot_general(
        rows, jnp.take(up, spots, axis=0), contract, preferred_element_type=jnp.float32
    )
    audio_block = lax.dot_general(
        audio, jnp.take(up, audio_spots, axis=0), contract, preferred_element_type=jnp.float32
    )
    merger = lax.psum_scatter(merger, ("y", "core"), tiled=True)
    audio_block = lax.psum_scatter(
        audio_block.reshape(GRID_ROWS, enc // GRID_ROWS, block_cols), ("y", "core"), tiled=True
    )
    return (merger[None], audio_block)


def solution(mesh):
    whole = Mesh(mesh.devices.reshape(8, 4, 4, 2), ("z", "x", "y", "core"))
    dp, ctx = (("y", "core"), ("z", "x"))
    return jax.shard_map(
        local,
        mesh=whole,
        in_specs=(
            P(dp, ctx, None),
            P(),
            P(),
            P(dp, ctx, None),
            P(dp, ctx),
            P(dp, ctx),
            P(dp, ctx),
            P(dp, ctx, None),
        ),
        out_specs=(P(ctx, dp, None), P(ctx, dp, None)),
        check_vma=False,
    )
```

profile of v0, /device:TPU:2, one launch (start us, length us, event | category | flops | bytes accessed | tf_op | source)
XLA Modules:
  0.0 306.2 jit_solution(9559356676186818272)
XLA Ops:
  7.2 13.5 %all_gather.43 = bf16[4,128,128]{2,1,0:T(8,128)(2,1)} all-gather(bf16[1,128,128]{2,1,0:T(8,128)(2,1)} %param.8), channel_id=1, replica_groups=mesh['z'=8,'x'=4,'y'=4,'core'=2] {'x'}, dimensions={0}, use_global_device_ids=true | all-gather | bytes 163840 | tf_op jit(solution)/shard_map/all_gather | solution.py:39
  20.8 2.8 reshape_squeeze.3
  23.7 20.1 %all_to_all.10 = bf16[4,192,896]{2,1,0:T(8,128)(2,1)} all-to-all(bf16[4,192,896]{2,1,0:T(8,128)(2,1)S(1)} %copy.21), channel_id=1, replica_groups=mesh['z'=8,'x'=4,'y'=4,'core'=2] {'x'}, dimensions={0} | all-to-all | bytes 2752512 | tf_op jit(solution)/shard_map/all_to_all | solution.py:19
  43.9 1.0 slice_bitcast_fusion.1
  46.1 9.9 %collective-permute-done = bf16[64,5120]{1,0:T(8,128)(2,1)S(1)} collective-permute-done((bf16[64,5120]{1,0:T(8,128)(2,1)}, bf16[64,5120]{1,0:T(8,128)(2,1)S(1)}, u32[]{:S(2)}, u32[]{:S(2)}) %collective-permute-start) | collective-permute-done | bytes 655392 | tf_op jit(solution)/shard_map/ppermute | solution.py:26
  56.9 1.2 pad_maximum_fusion
  58.1 0.9 gather_fusion
  59.1 1.0 fusion.58
  60.1 9.3 %all-to-all-start = ((bf16[8,64,640]{2,1,0:T(8,128)(2,1)}), bf16[8,64,640]{2,1,0:T(8,128)(2,1)S(1)}, u32[]{:S(2)}, u32[]{:S(2)}) async-start(bf16[8,64,640]{2,1,0:T(8,128)(2,1)} %fusion.58), calls=%async_computation | async-start | bytes 1310720 | tf_op jit(solution)/shard_map/all_to_all | solution.py:33
  69.6 1.5 collective-permute-start.1
  71.1 7.5 %all-gather.6 = s32[4,1,128]{2,1,0:T(1,128)S(1)} all-gather(s32[1,1,128]{2,1,0:T(1,128)S(1)} %bitcast.54), channel_id=1, replica_groups=mesh['z'=8,'x'=4,'y'=4,'core'=2] {'x'}, dimensions={0}, use_global_device_ids=true | all-gather | bytes 2560 | tf_op jit(solution)/shard_map/all_gather | solution.py:40
  78.5 25.6 %all-gather.7 = s32[8,4,128]{2,1,0:T(4,128)S(1)} all-gather(s32[1,4,128]{2,1,0:T(4,128)S(1)} %bitcast.53), channel_id=5, replica_groups=mesh['z'=8,'x'=4,'y'=4,'core'=2] {'z'}, dimensions={0}, use_global_device_ids=true | all-gather | bytes 18432 | tf_op jit(solution)/shard_map/all_gather | solution.py:40
  106.8 8.8 %all-gather.4 = s32[4,1,64]{2,1,0:T(1,128)S(1)} all-gather(s32[1,1,64]{2,1,0:T(1,128)S(1)} %fusion.62), channel_id=1, replica_groups=mesh['z'=8,'x'=4,'y'=4,'core'=2] {'x'}, dimensions={0}, use_global_device_ids=true | all-gather | bytes 1280 | tf_op jit(solution)/shard_map/all_gather | solution.py:38
  115.6 21.3 %all-gather.5 = s32[8,4,64]{2,1,0:T(4,128)S(1)} all-gather(s32[1,4,64]{2,1,0:T(4,128)S(1)} %bitcast.52), channel_id=3, replica_groups=mesh['z'=8,'x'=4,'y'=4,'core'=2] {'z'}, dimensions={0}, use_global_device_ids=true | all-gather | bytes 9216 | tf_op jit(solution)/shard_map/all_gather | solution.py:38
  137.0 3.1 %pad_slice_fusion.1 = (bf16[4096,128]{1,0:T(8,128)(2,1)S(1)}, bf16[4096,128]{1,0:T(8,128)(2,1)}) fusion(bf16[4096,128]{1,0:T(8,128)(2,1)} %bitcast.46), kind=kLoop, calls=%fused_computation.69 | loop fusion | bytes 3145728 | tf_op jit(solution)/shard_map/slice | solution.py:43
  140.1 47.5 %all-gather.12.cloned.1.call-done = bf16[32,192,896]{2,1,0:T(8,128)(2,1)} async-done(((bf16[4,192,896]{2,1,0:T(8,128)(2,1)}), bf16[32,192,896]{2,1,0:T(8,128)(2,1)}) %all-gather.12.cloned.1.call-update) | async-done | bytes 11010064 | tf_op jit(solution)/shard_map/all_gather | solution.py:22
  187.7 25.4 %gather_fusion.3 = bf16[4096,896]{1,0:T(8,128)(2,1)} fusion(bf16[6144,896]{1,0:T(8,128)(2,1)} %bitcast.42, s32[4096]{0:T(1024)S(1)} %broadcast_clamp_fusion), kind=kCustom, calls=%fused_computation.3 | custom fusion | bytes 14696448 | tf_op jit(solution)/shard_map/jit(_take)/gather | solution.py:53
  213.1 13.1 %fusion = f32[160,896]{1,0:T(8,128)} fusion(bf16[4096,896]{1,0:T(8,128)(2,1)} %gather_fusion.3, pred[4096]{0:T(1024)(128)(4,1)S(1)} %compare_and_fusion, bf16[4096,128]{1,0:T(8,128)(2,1)} %get-tuple-element.13, bf16[4096,128]{1,0:T(8,128)(2,1)S(1)} %bitcast.47, bf16[4096,128]{1,0:T(8,128)(2,1)S(1)} %get-tuple-element.12, f32[160]{0:T(256)S(1)} %dynamic_slice.7, ...), kind=kOutput, calls=%fused_computation.4 | convolution fusion | flops 1734082560 | bytes 11260932 | tf_op jit(solution)/shard_map/dot_general | solution.py:52
  226.3 2.0 reshape.201
  228.7 16.0 %gather_fusion.2 = bf16[2048,896]{1,0:T(8,128)(2,1)} fusion(bf16[6144,896]{1,0:T(8,128)(2,1)} %bitcast.43, s32[2048]{0:T(1024)S(1)} %broadcast_clamp_fusion.1), kind=kCustom, calls=%fused_computation.2 | custom fusion | bytes 7348224 | tf_op jit(solution)/shard_map/jit(_take)/gather | solution.py:50
  244.7 7.2 %fusion.4 = f32[640,896]{1,0:T(8,128)} fusion(bf16[2048,640]{1,0:T(8,128)(2,1)} %bitcast.55, bf16[2048,896]{1,0:T(8,128)(2,1)} %gather_fusion.2, pred[2048]{0:T(1024)(128)(4,1)S(1)} %compare_and_fusion.1), kind=kOutput, calls=%fused_computation.10 | convolution fusion | flops 2350645248 | bytes 8587264 | tf_op jit(solution)/shard_map/dot_general | solution.py:49
  251.9 9.3 %reduce-scatter.7.cloned.1.call-done = f32[1,20,896]{2,1,0:T(8,128)} async-done(((f32[8,20,896]{2,1,0:T(8,128)}), f32[1,20,896]{2,1,0:T(8,128)}) %reduce-scatter.7.cloned.1.call-update) | async-done | bytes 71696
  261.2 1.6 copy.22
  262.8 36.9 %reduce-scatter.5.cloned.1.call-done = f32[80,896]{1,0:T(8,128)} async-done(((f32[640,896]{1,0:T(8,128)}), f32[80,896]{1,0:T(8,128)}) %reduce-scatter.5.cloned.1.call-update) | async-done | bytes 286736 | tf_op jit(solution)/shard_map/reduce_scatter | solution.py:55
  (46 shorter events, 5.0 us)
Async XLA Ops:
  7.2 206.0 %copy-start = (bf16[384,1280]{1,0:T(8,128)(2,1)S(1)}, bf16[384,1280]{1,0:T(8,128)(2,1)}, u32[]{:S(2)}) copy-start(bf16[384,1280]{1,0:T(8,128)(2,1)} %param.9) | copy-start | bytes 2949124
  7.2 129.9 %all-gather.16.cloned.1.call-start = ((), (), s32[]{:S(2)}) async-start(), calls=%async_computation.7 | async-start | bytes 1179648 | tf_op jit(solution)/shard_map/all_gather | solution.py:39
  20.7 166.9 %all-gather.12.cloned.1.call-start = ((), (), s32[]{:S(2)}) async-start(), calls=%async_computation.4 | async-start | bytes 12386304 | tf_op jit(solution)/shard_map/all_gather | solution.py:22
  23.7 20.1 %copy-start.2 = (bf16[1,128,5120]{2,1,0:T(8,128)(2,1)S(1)}, bf16[1,128,5120]{2,1,0:T(8,128)(2,1)}, u32[]{:S(2)}) copy-start(bf16[1,128,5120]{2,1,0:T(8,128)(2,1)} %param.11) | copy-start | bytes 3932164
  44.8 11.2 %collective-permute-start = (bf16[64,5120]{1,0:T(8,128)(2,1)}, bf16[64,5120]{1,0:T(8,128)(2,1)S(1)}, u32[]{:S(2)}, u32[]{:S(2)}) collective-permute-start(bf16[64,5120]{1,0:T(8,128)(2,1)} %get-tuple-element.11), channel_id=1, source_target_pairs={{0,8},{8,0},{16,24},{24,16},{1,9},{9,1},{17,25},{25,17},{2,10},{10... | collective-permute-start | bytes 1966088 | tf_op jit(solution)/shard_map/ppermute | solution.py:26
  56.0 0.9 copy-start.4
  59.0 10.4 %copy-start.5 = (s32[1,128]{1,0:T(1,128)S(1)}, s32[1,128]{1,0:T(1,128)}, u32[]{:S(2)}) copy-start(s32[1,128]{1,0:T(1,128)} %param.13) | copy-start | bytes 1540
  59.1 12.0 %copy-start.6 = (s32[1,128]{1,0:T(1,128)S(1)}, s32[1,128]{1,0:T(1,128)}, u32[]{:S(2)}) copy-start(s32[1,128]{1,0:T(1,128)} %param.14) | copy-start | bytes 1540
  60.1 44.1 %all-to-all-start = ((bf16[8,64,640]{2,1,0:T(8,128)(2,1)}), bf16[8,64,640]{2,1,0:T(8,128)(2,1)S(1)}, u32[]{:S(2)}, u32[]{:S(2)}) async-start(bf16[8,64,640]{2,1,0:T(8,128)(2,1)} %fusion.58), calls=%async_computation | async-start | bytes 1310720 | tf_op jit(solution)/shard_map/all_to_all | solution.py:33
  69.4 175.2 %all-gather.14.cloned.1.call-start = ((), (), s32[]{:S(2)}) async-start(), calls=%async_computation.6 | async-start | bytes 3276800 | tf_op jit(solution)/shard_map/all_gather | solution.py:36
  69.6 36.4 %collective-permute-start.1 = (s32[64]{0:T(128)S(1)}, s32[64]{0:T(128)S(1)}, u32[]{:S(2)}, u32[]{:S(2)}) collective-permute-start(s32[64]{0:T(128)S(1)} %get-tuple-element.15), channel_id=1, source_target_pairs={{0,8},{8,0},{16,24},{24,16},{1,9},{9,1},{17,25},{25,17},{2,10},{10... | collective-permute-start | bytes 776 | tf_op jit(solution)/shard_map/ppermute | solution.py:26
  104.2 0.9 copy-start.1
  105.1 156.1 %reduce-scatter.7.cloned.1.call-start = ((), (), s32[]{:S(2)}) async-start(), calls=%async_computation.8 | async-start | bytes 774144
  187.7 25.5 %copy-start.3 = (bf16[32,128,128]{2,1,0:T(8,128)(2,1)S(1)}, bf16[32,128,128]{2,1,0:T(8,128)(2,1)}, u32[]{:S(2)}) copy-start(bf16[32,128,128]{2,1,0:T(8,128)(2,1)} %all-gather.16.cloned.1.call-done) | copy-start | bytes 3145732
  228.3 71.4 %reduce-scatter.5.cloned.1.call-start = ((), (), s32[]{:S(2)}) async-start(), calls=%async_computation.5 | async-start | bytes 2580480 | tf_op jit(solution)/shard_map/reduce_scatter | solution.py:55
Sparse Core Ops, SparseCore 0:
  20.9 40.8 all-gather.15
  63.5 124.1 all-gather.11
  189.5 34.3 all-gather.13
  228.4 32.7 reduce-scatter.6
  264.2 35.4 reduce-scatter.4
where the time goes:
time: 307 us; the launch traced here: 306 us
  waiting for transfers between devices  104 us (34%)
  blocking collectives  96.8 us (32%)
  local copies, waits for them, and re-layouts  56.5 us (18%)
  matrix products  20.3 us (7%)
  between operations  14.6 us (5%)
  starting transfers between devices  11.8 us (4%)
    all_gather x1, waiting for transfers between devices, local(): up = lax.all_gather(cols, 'z', tiled=True).reshape(-1, block_cols)  47.5 us
    reduce_scatter x1, waiting for transfers between devices, local(): merger = lax.psum_scatter(merger, ('y', 'core'), tiled=True)  36.9 us
    all_gather x2, blocking collectives, local(): spots = lax.all_gather(lax.all_gather(spots, 'x'), 'z').reshape(-1)  30.1 us
    all_gather x1, blocking collectives, local(): lax.all_gather(lax.all_gather(audio_places[0], 'x'), 'z').reshape(-1)  25.6 us
    gather x1, local copies, waits for them, and re-layouts, local(): jnp.take(up, audio_spots, axis=0)  25.4 us
    all_to_all x1, blocking collectives, local(): lax.all_to_all(jnp.transpose(upstream.reshape(-1, GRID_COLS, block_cols),...  20.1 us
    gather x1, local copies, waits for them, and re-layouts, local(): jnp.take(up, spots, axis=0)  16 us
    all_gather x1, blocking collectives, local(): lax.all_gather(mel[0], 'x')  13.5 us
  transfers between devices with their start and end apart: 8, of which 4 were waited for; matrix products, arithmetic and copies ran while one was open for 25% of the time, Pallas kernels for 0%

commit v1 on v0

--- a/solution.py
+++ b/solution.py
@@ -19,7 +19,15 @@
     cols = lax.all_to_all(
         jnp.transpose(upstream.reshape(-1, GRID_COLS, block_cols), (1, 0, 2)), "x", 0, 0, tiled=True
     )
-    up = lax.all_gather(cols, "z", tiled=True).reshape(-1, block_cols)
+    up = jnp.concatenate(
+        lax.all_to_all(
+            jnp.stack([cols for _ in range(lax.psum(1, axis_name="z"))], axis=0),
+            split_axis=0,
+            concat_axis=0,
+            axis_name="z",
+        ),
+        0,
+    ).reshape(-1, block_cols)
     live_count = video_count[0, 0]
     middle = hidden.shape[0] // 2
     pairs = [(i, i ^ 1) for i in range(lax.axis_size("x"))]

time: 307 us -> 497 us (1.62)
  blocking collectives: 96.8 us -> 317 us
  waiting for transfers between devices: 104 us -> 63.7 us
  local copies, waits for them, and re-layouts: 56.5 us -> 64.1 us
    all_gather x1, blocking collectives: 25.6 us -> 240 us  [local(): lax.all_gather(lax.all_gather(audio_places[0], 'x'), 'z').reshape(-1)]
    all_gather x1 -> x0, waiting for transfers between devices: 47.5 us -> none  [local(): up = lax.all_gather(cols, 'z', tiled=True).reshape(-1, block_cols)]
    all_to_all x1 -> x2, waiting for transfers between devices: 0.01 us -> 12 us  [the longest x1 12 us: local(): lax.all_to_all(jnp.transpose(upstream.reshape(-1, GRID_COLS, block_cols),...]
    all_to_all x1, blocking collectives: 20.1 us -> 27.8 us  [local(): lax.all_to_all(jnp.transpose(rows.reshape(middle, GRID_ROWS, -1), (1, 0,...]
    another operation x0 -> x1, local copies, waits for them, and re-layouts: none -> 6.94 us  [local(): jnp.stack([cols for _ in range(lax.psum(1, axis_name='z'))], axis=0)]
  transfers between devices with their start and end apart: 8 -> 8, of which waited for: 4 -> 4; matrix products, arithmetic and copies ran while one was open for 25% -> 15% of each run, Pallas kernels for 0% -> 0%
where the time goes in v1:
time: 497 us; the launch traced here: 496 us
  blocking collectives  317 us (64%)
  local copies, waits for them, and re-layouts  64.1 us (13%)
  waiting for transfers between devices  63.7 us (13%)
  matrix products  20.3 us (4%)
  starting transfers between devices  15 us (3%)
  between operations  14.6 us (3%)
    all_gather x1, blocking collectives, local(): lax.all_gather(lax.all_gather(audio_places[0], 'x'), 'z').reshape(-1)  240 us
    reduce_scatter x1, waiting for transfers between devices, local(): merger = lax.psum_scatter(merger, ('y', 'core'), tiled=True)  36.9 us
    all_gather x2, blocking collectives, local(): spots = lax.all_gather(lax.all_gather(spots, 'x'), 'z').reshape(-1)  30.1 us
    all_to_all x1, blocking collectives, local(): lax.all_to_all(jnp.transpose(rows.reshape(middle, GRID_ROWS, -1), (1, 0,...  27.8 us
    gather x1, local copies, waits for them, and re-layouts, local(): jnp.take(up, audio_spots, axis=0)  25.5 us
    gather x1, local copies, waits for them, and re-layouts, local(): jnp.take(up, spots, axis=0)  16 us
    dot_general x1, matrix products, local(): lax.dot_general(audio, jnp.take(up, audio_spots, axis=0), contract, prefe...  13.1 us
    all_to_all x1, waiting for transfers between devices, local(): lax.all_to_all(jnp.transpose(upstream.reshape(-1, GRID_COLS, block_cols),...  12 us
  transfers between devices with their start and end apart: 8, of which 4 were waited for; matrix products, arithmetic and copies ran while one was open for 15% of the time, Pallas kernels for 0%

profile of v1, /device:TPU:2, one launch (start us, length us, event | category | flops | bytes accessed | tf_op | source)
XLA Modules:
  0.0 496.4 jit_solution(13168555314223649793)
XLA Ops:
  7.2 2.3 slice_bitcast_fusion.1
  9.5 2.3 collective-permute-start
  11.7 2.8 reshape_squeeze.3
  15.8 4.3 all-to-all-start.1
  20.8 6.9 %collective-permute-done = bf16[64,5120]{1,0:T(8,128)(2,1)} collective-permute-done((bf16[64,5120]{1,0:T(8,128)(2,1)}, bf16[64,5120]{1,0:T(8,128)(2,1)}, u32[]{:S(2)}, u32[]{:S(2)}) %collective-permute-start) | collective-permute-done | bytes 655392 | tf_op jit(solution)/shard_map/ppermute | solution.py:34
  30.0 12.0 %all-to-all-done.1 = bf16[4,192,896]{2,1,0:T(8,128)(2,1)} async-done(((bf16[4,192,896]{2,1,0:T(8,128)(2,1)}), bf16[4,192,896]{2,1,0:T(8,128)(2,1)}, u32[]{:S(2)}, u32[]{:S(2)}) %all-to-all-start.1) | async-done | bytes 1376288 | tf_op jit(solution)/shard_map/all_to_all | solution.py:19
  41.9 27.8 %all_to_all.15 = bf16[8,64,640]{2,1,0:T(8,128)(2,1)} all-to-all(bf16[8,64,640]{2,1,0:T(8,128)(2,1)S(1)} %fusion.58), channel_id=1, replica_groups=mesh['z'=8,'x'=4,'y'=4,'core'=2] {'z'}, dimensions={0} | all-to-all | bytes 1310720 | tf_op jit(solution)/shard_map/all_to_all | solution.py:41
  69.7 6.9 %stack.2 = bf16[8,4,192,896]{3,2,1,0:T(8,128)(2,1)} broadcast(bf16[4,192,896]{2,1,0:T(8,128)(2,1)} %all-to-all-done.1), dimensions={1,2,3} | broadcast | bytes 12386304 | tf_op jit(solution)/shard_map/stack | solution.py:24
  76.7 5.3 %all-to-all-start.2 = ((bf16[8,4,192,896]{3,2,1,0:T(8,128)(2,1)}), bf16[8,4,192,896]{3,2,1,0:T(8,128)(2,1)}, u32[]{:S(2)}, u32[]{:S(2)}) async-start(bf16[8,4,192,896]{3,2,1,0:T(8,128)(2,1)} %stack.2), calls=%async_computation.2 | async-start | bytes 22020096 | tf_op jit(solution)/shard_map/all_to_all | solution.py:23
  82.1 11.9 %all_gather.39 = bf16[4,128,128]{2,1,0:T(8,128)(2,1)} all-gather(bf16[1,128,128]{2,1,0:T(8,128)(2,1)S(1)} %copy-done.2), channel_id=1, replica_groups=mesh['z'=8,'x'=4,'y'=4,'core'=2] {'x'}, dimensions={0}, use_global_device_ids=true | all-gather | bytes 163840 | tf_op jit(solution)/shard_map/all_gather | solution.py:47
  94.1 2.7 collective-permute-start.1
  96.8 6.9 %all-gather.6 = s32[4,1,128]{2,1,0:T(1,128)S(1)} all-gather(s32[1,1,128]{2,1,0:T(1,128)S(1)} %bitcast.52), channel_id=1, replica_groups=mesh['z'=8,'x'=4,'y'=4,'core'=2] {'x'}, dimensions={0}, use_global_device_ids=true | all-gather | bytes 2560 | tf_op jit(solution)/shard_map/all_gather | solution.py:48
  103.7 240.5 %all-gather.7 = s32[8,4,128]{2,1,0:T(4,128)S(1)} all-gather(s32[1,4,128]{2,1,0:T(4,128)S(1)} %bitcast.51), channel_id=5, replica_groups=mesh['z'=8,'x'=4,'y'=4,'core'=2] {'z'}, dimensions={0}, use_global_device_ids=true | all-gather | bytes 18432 | tf_op jit(solution)/shard_map/all_gather | solution.py:48
  346.0 8.7 %all-gather.4 = s32[4,1,64]{2,1,0:T(1,128)S(1)} all-gather(s32[1,1,64]{2,1,0:T(1,128)S(1)} %fusion.62), channel_id=1, replica_groups=mesh['z'=8,'x'=4,'y'=4,'core'=2] {'x'}, dimensions={0}, use_global_device_ids=true | all-gather | bytes 1280 | tf_op jit(solution)/shard_map/all_gather | solution.py:46
  354.7 21.3 %all-gather.5 = s32[8,4,64]{2,1,0:T(4,128)S(1)} all-gather(s32[1,4,64]{2,1,0:T(4,128)S(1)} %bitcast.50), channel_id=3, replica_groups=mesh['z'=8,'x'=4,'y'=4,'core'=2] {'z'}, dimensions={0}, use_global_device_ids=true | all-gather | bytes 9216 | tf_op jit(solution)/shard_map/all_gather | solution.py:46
  376.1 3.1 pad_slice_fusion.1
  379.3 25.5 %gather_fusion.3 = bf16[4096,896]{1,0:T(8,128)(2,1)} fusion(bf16[6144,896]{1,0:T(8,128)(2,1)} %bitcast.12, s32[4096]{0:T(1024)S(1)} %broadcast_clamp_fusion), kind=kCustom, calls=%fused_computation.3 | custom fusion | bytes 14696448 | tf_op jit(solution)/shard_map/jit(_take)/gather | solution.py:61
  404.7 13.1 %fusion = f32[160,896]{1,0:T(8,128)} fusion(bf16[4096,896]{1,0:T(8,128)(2,1)} %gather_fusion.3, pred[4096]{0:T(1024)(128)(4,1)S(1)} %compare_and_fusion, bf16[4096,128]{1,0:T(8,128)(2,1)} %get-tuple-element.11, bf16[4096,128]{1,0:T(8,128)(2,1)S(1)} %bitcast.45, bf16[4096,128]{1,0:T(8,128)(2,1)S(1)} %get-tuple-element.10, f32[160]{0:T(256)S(1)} %dynamic_slice.7, ...), kind=kOutput, calls=%fused_computation.4 | convolution fusion | flops 1734082560 | bytes 11260932 | tf_op jit(solution)/shard_map/dot_general | solution.py:60
  417.9 2.0 reshape.199
  420.2 16.0 %gather_fusion.2 = bf16[2048,896]{1,0:T(8,128)(2,1)} fusion(bf16[6144,896]{1,0:T(8,128)(2,1)} %bitcast.12, s32[2048]{0:T(1024)S(1)} %broadcast_clamp_fusion.1), kind=kCustom, calls=%fused_computation.2 | custom fusion | bytes 7348224 | tf_op jit(solution)/shard_map/jit(_take)/gather | solution.py:58
  436.3 7.2 %fusion.4 = f32[640,896]{1,0:T(8,128)} fusion(bf16[2048,640]{1,0:T(8,128)(2,1)} %bitcast.53, bf16[2048,896]{1,0:T(8,128)(2,1)} %gather_fusion.2, pred[2048]{0:T(1024)(128)(4,1)S(1)} %compare_and_fusion.1), kind=kOutput, calls=%fused_computation.10 | convolution fusion | flops 2350645248 | bytes 8587264 | tf_op jit(solution)/shard_map/dot_general | solution.py:57
  443.5 7.9 %reduce-scatter.7.cloned.1.call-done = f32[1,20,896]{2,1,0:T(8,128)} async-done(((f32[8,20,896]{2,1,0:T(8,128)}), f32[1,20,896]{2,1,0:T(8,128)}) %reduce-scatter.7.cloned.1.call-update) | async-done | bytes 71696
  451.4 1.6 copy.19
  453.0 36.9 %reduce-scatter.5.cloned.1.call-done = f32[80,896]{1,0:T(8,128)} async-done(((f32[640,896]{1,0:T(8,128)}), f32[80,896]{1,0:T(8,128)}) %reduce-scatter.5.cloned.1.call-update) | async-done | bytes 286736 | tf_op jit(solution)/shard_map/reduce_scatter | solution.py:63
  (42 shorter events, 5.9 us)
Async XLA Ops:
  7.2 397.6 %copy-start = (bf16[384,1280]{1,0:T(8,128)(2,1)S(1)}, bf16[384,1280]{1,0:T(8,128)(2,1)}, u32[]{:S(2)}) copy-start(bf16[384,1280]{1,0:T(8,128)(2,1)} %param.9) | copy-start | bytes 2949124
  9.5 18.2 %collective-permute-start = (bf16[64,5120]{1,0:T(8,128)(2,1)}, bf16[64,5120]{1,0:T(8,128)(2,1)}, u32[]{:S(2)}, u32[]{:S(2)}) collective-permute-start(bf16[64,5120]{1,0:T(8,128)(2,1)} %get-tuple-element.9), channel_id=1, source_target_pairs={{0,8},{8,0},{16,24},{24,16},{1,9},{9,1},{17,25},{25,17},{2,10},{10... | collective-permute-start | bytes 1966088 | tf_op jit(solution)/shard_map/ppermute | solution.py:34
  15.8 26.2 %all-to-all-start.1 = ((bf16[4,192,896]{2,1,0:T(8,128)(2,1)}), bf16[4,192,896]{2,1,0:T(8,128)(2,1)}, u32[]{:S(2)}, u32[]{:S(2)}) async-start(bf16[4,192,896]{2,1,0:T(8,128)(2,1)} %copy.18), calls=%async_computation.1 | async-start | bytes 2752512 | tf_op jit(solution)/shard_map/all_to_all | solution.py:19
  76.7 5.4 %copy-start.2 = (bf16[1,128,128]{2,1,0:T(8,128)(2,1)S(1)}, bf16[1,128,128]{2,1,0:T(8,128)(2,1)}, u32[]{:S(2)}) copy-start(bf16[1,128,128]{2,1,0:T(8,128)(2,1)} %param.8) | copy-start | bytes 98308
  76.7 17.4 %copy-start.3 = (s32[1,128]{1,0:T(1,128)S(1)}, s32[1,128]{1,0:T(1,128)}, u32[]{:S(2)}) copy-start(s32[1,128]{1,0:T(1,128)} %param.13) | copy-start | bytes 1540
  76.7 20.1 %copy-start.4 = (s32[1,128]{1,0:T(1,128)S(1)}, s32[1,128]{1,0:T(1,128)}, u32[]{:S(2)}) copy-start(s32[1,128]{1,0:T(1,128)} %param.14) | copy-start | bytes 1540
  76.7 302.6 %all-to-all-start.2 = ((bf16[8,4,192,896]{3,2,1,0:T(8,128)(2,1)}), bf16[8,4,192,896]{3,2,1,0:T(8,128)(2,1)}, u32[]{:S(2)}, u32[]{:S(2)}) async-start(bf16[8,4,192,896]{3,2,1,0:T(8,128)(2,1)} %stack.2), calls=%async_computation.2 | async-start | bytes 22020096 | tf_op jit(solution)/shard_map/all_to_all | solution.py:23
  82.0 294.1 %all-gather.13.cloned.1.call-start = ((), (), s32[]{:S(2)}) async-start(), calls=%async_computation.7 | async-start | bytes 1179648 | tf_op jit(solution)/shard_map/all_gather | solution.py:47
  94.0 342.3 %all-gather.11.cloned.1.call-start = ((), (), s32[]{:S(2)}) async-start(), calls=%async_computation.6 | async-start | bytes 3276800 | tf_op jit(solution)/shard_map/all_gather | solution.py:44
  94.1 251.0 %collective-permute-start.1 = (s32[64]{0:T(128)S(1)}, s32[64]{0:T(128)S(1)}, u32[]{:S(2)}, u32[]{:S(2)}) collective-permute-start(s32[64]{0:T(128)S(1)} %get-tuple-element.13), channel_id=1, source_target_pairs={{0,8},{8,0},{16,24},{24,16},{1,9},{9,1},{17,25},{25,17},{2,10},{10... | collective-permute-start | bytes 776 | tf_op jit(solution)/shard_map/ppermute | solution.py:34
  344.2 107.1 %reduce-scatter.7.cloned.1.call-start = ((), (), s32[]{:S(2)}) async-start(), calls=%async_computation.8 | async-start | bytes 774144
  379.3 25.5 %copy-start.1 = (bf16[32,128,128]{2,1,0:T(8,128)(2,1)S(1)}, bf16[32,128,128]{2,1,0:T(8,128)(2,1)}, u32[]{:S(2)}) copy-start(bf16[32,128,128]{2,1,0:T(8,128)(2,1)} %all-gather.13.cloned.1.call-done) | copy-start | bytes 3145732
  419.9 70.0 %reduce-scatter.5.cloned.1.call-start = ((), (), s32[]{:S(2)}) async-start(), calls=%async_computation.5 | async-start | bytes 2580480 | tf_op jit(solution)/shard_map/reduce_scatter | solution.py:63
Sparse Core Ops, SparseCore 0:
  94.1 57.3 all-gather.12
  344.3 35.3 all-gather.10
  420.0 31.3 reduce-scatter.6
  454.4 35.4 reduce-scatter.4
